TPU v7x, 32 devices: a whole 2x2x4 slice. The times are simulated.
32 devices in a mesh: section: 2 (over y), ctx: 16 (over z, x, core).
Axes of the slice: x: 2, y: 2, z: 4, core: 2. Of those that a mesh axis runs over, the one named last changes fastest.
Arguments:
- query_rows: bfloat16 [2, 2048, 896], P('section', 'ctx'), may hold values from -6 to 6
- key_rows: bfloat16 [2, 2048, 128], P('section', 'ctx'), may hold values from -6 to 6
- value_rows: bfloat16 [2, 2048, 128], P('section', 'ctx'), may hold values from -6 to 6
- attn_output: bfloat16 [2, 2048, 896], P('section', 'ctx'), may hold values from -6 to 6
- grad_output: bfloat16 [2, 2048, 896], P('section', 'ctx'), may hold values from -24 to 24
- log_normalizer: float32 [2, 7, 2048], P('section', None, 'ctx'), as said below
- positions: int32 [2048], P('ctx'), may hold values from 0 to 2047, as said below
Outputs:
- grad_query: bfloat16 [2, 2048, 896], P('section', 'ctx')
- grad_key: bfloat16 [2, 2048, 128], P('section', 'ctx')
- grad_value: bfloat16 [2, 2048, 128], P('section', 'ctx')
Inputs may be any that keep to these rules, and one draw needn't show every extreme that they name: Each of 0 to 2047 appears once. The positions are cut into 32 runs of 64 consecutive positions; the rows of each device of ctx hold run r and then run 32 - 1 - r, each ascending, where which r a device holds is drawn, one device for each r. `log_normalizer`: within 0.5 of log(1 + the row's position) + 1.
All inputs are finite; a program needn't handle non-finite values.
Results may differ from a plain program's by a relative error of at most 0.0051.
Values may be sent and summed in bfloat16 or wider, within the bound.
A program may use at most 64 MiB of HBM per device.

v0:
```python
import jax
import jax.numpy as jnp
from jax import lax
from jax.sharding import PartitionSpec as P


def from_behind(block, axis, distance):
    devices = range(lax.axis_size(axis))
    route = [((i - distance) % len(devices), i) for i in devices]
    return lax.ppermute(block, axis, route)


def tile_terms(
    query_part, grad_part, dot_part, norm_part, query_pos, key_part, value_part, key_pos, scaling
):
    scores = (
        jnp.einsum("ihd,jd->hij", query_part, key_part, preferred_element_type=jnp.float32)
        * scaling
    )
    allowed = key_pos[None, :] <= query_pos[:, None]
    probs = jnp.where(allowed[None], jnp.exp(scores - norm_part[:, :, None]), 0.0)
    grad_probs = jnp.einsum(
        "ihd,jd->hij", grad_part, value_part, preferred_element_type=jnp.float32
    )
    grad_scores = (probs * (grad_probs - dot_part[:, :, None])).astype(jnp.bfloat16)
    probs_low = probs.astype(jnp.bfloat16)
    query_grad = (
        jnp.einsum("hij,jd->ihd", grad_scores, key_part, preferred_element_type=jnp.float32)
        * scaling
    )
    key_grad = (
        jnp.einsum("hij,ihd->jd", grad_scores, query_part, preferred_element_type=jnp.float32)
        * scaling
    )
    value_grad = jnp.einsum("hij,ihd->jd", probs_low, grad_part, preferred_element_type=jnp.float32)
    return (query_grad, key_grad, value_grad)


def block_terms(local_data, key_part, value_part, key_pos):
    query3, grad3, grad_dot, log_norm, query_pos, scaling = local_data
    row_count = query3.shape[0]
    half_rows = row_count // 2
    group_size = query3.shape[1]
    head_width = query3.shape[2]
    key_sums = [jnp.zeros((half_rows, head_width), jnp.float32) for _ in range(2)]
    value_sums = [jnp.zeros((half_rows, head_width), jnp.float32) for _ in range(2)]
    query_halves = []

    def compute(operands):
        return tile_terms(*operands, scaling)

    def nothing(operands):
        return (
            jnp.zeros((half_rows, group_size, head_width), jnp.float32),
            jnp.zeros((half_rows, head_width), jnp.float32),
            jnp.zeros((half_rows, head_width), jnp.float32),
        )

    for query_half in range(2):
        query_slice = slice(query_half * half_rows, (query_half + 1) * half_rows)
        total_query = jnp.zeros((half_rows, group_size, head_width), jnp.float32)
        for key_half in range(2):
            key_slice = slice(key_half * half_rows, (key_half + 1) * half_rows)
            masked_out = jnp.min(key_pos[key_slice]) > jnp.max(query_pos[query_slice])
            operands = (
                query3[query_slice],
                grad3[query_slice],
                grad_dot[:, query_slice],
                log_norm[:, query_slice],
                query_pos[query_slice],
                key_part[key_slice],
                value_part[key_slice],
                key_pos[key_slice],
            )
            part_query, part_key, part_value = lax.cond(masked_out, nothing, compute, operands)
            total_query = total_query + part_query
            key_sums[key_half] = key_sums[key_half] + part_key
            value_sums[key_half] = value_sums[key_half] + part_value
        query_halves.append(total_query)
    return (
        jnp.concatenate(query_halves, axis=0),
        jnp.concatenate(key_sums, axis=0),
        jnp.concatenate(value_sums, axis=0),
    )


def shards(query_rows, key_rows, value_rows, attn_output, grad_output, log_normalizer, positions):
    row_count = query_rows.shape[1]
    head_width = key_rows.shape[2]
    group_size = query_rows.shape[2] // head_width
    scaling = head_width ** (-0.5)
    query3 = query_rows[0].reshape(row_count, group_size, head_width)
    grad3 = grad_output[0].reshape(row_count, group_size, head_width)
    out3 = attn_output[0].reshape(row_count, group_size, head_width)
    grad_dot = jnp.sum(grad3.astype(jnp.float32) * out3.astype(jnp.float32), axis=2).T
    log_norm = log_normalizer[0]
    all_positions = lax.all_gather(positions, "ctx", axis=0, tiled=True)
    cycle_size = lax.axis_size("ctx")
    cycle_index = lax.axis_index("ctx")
    local_data = (query3, grad3, grad_dot, log_norm, positions, scaling)
    own_blocks = (key_rows[0], value_rows[0])
    zero_rows = jnp.zeros((row_count, head_width), jnp.float32)
    zero_query = jnp.zeros((row_count, group_size, head_width), jnp.float32)

    def key_positions(source):
        start = jnp.mod(source, cycle_size) * row_count
        return lax.dynamic_slice_in_dim(all_positions, start, row_count, 0)

    def process(carry_query, blocks, carried_grads, source):
        part_query, part_key, part_value = block_terms(
            local_data, blocks[0], blocks[1], key_positions(source)
        )
        return (
            carry_query + part_query,
            (carried_grads[0] + part_key, carried_grads[1] + part_value),
        )

    half_cycle = cycle_size // 2

    def two_step(step_index, loop_state):
        carry_query, ahead_blocks, ahead_grads, behind_blocks, behind_grads = loop_state
        behind_blocks = from_behind((behind_blocks[0], behind_blocks[1]), "ctx", -1)
        behind_grads = from_behind((behind_grads[0], behind_grads[1]), "ctx", -1)
        carry_query, ahead_grads = process(
            carry_query, ahead_blocks, ahead_grads, cycle_index - step_index
        )
        carry_query, behind_grads = process(
            carry_query, behind_blocks, behind_grads, cycle_index + 1 + step_index
        )
        ahead_blocks = from_behind((ahead_blocks[0], ahead_blocks[1]), "ctx", 1)
        ahead_grads = from_behind((ahead_grads[0], ahead_grads[1]), "ctx", 1)
        return (carry_query, ahead_blocks, ahead_grads, behind_blocks, behind_grads)

    start_state = (
        zero_query,
        own_blocks,
        (zero_rows, zero_rows),
        own_blocks,
        (zero_rows, zero_rows),
    )
    carry_query, ahead_blocks, ahead_grads, behind_blocks, behind_grads = lax.fori_loop(
        0, half_cycle, two_step, start_state
    )
    summed = (ahead_grads[0] + behind_grads[0], ahead_grads[1] + behind_grads[1])
    finished = (
        from_behind(summed[0].astype(jnp.bfloat16), "ctx", half_cycle).astype(jnp.float32),
        from_behind(summed[1].astype(jnp.bfloat16), "ctx", half_cycle).astype(jnp.float32),
    )
    query_grad = carry_query.reshape(row_count, group_size * head_width).astype(jnp.bfloat16)
    handed = from_behind(
        (query_grad, finished[0].astype(jnp.bfloat16), finished[1].astype(jnp.bfloat16)),
        "section",
        -1,
    )
    return (handed[0][None], handed[1][None], handed[2][None])


def solution(mesh):
    return jax.shard_map(
        shards,
        mesh=mesh,
        in_specs=(
            P("section", "ctx", None),
            P("section", "ctx", None),
            P("section", "ctx", None),
            P("section", "ctx", None),
            P("section", "ctx", None),
            P("section", None, "ctx"),
            P("ctx"),
        ),
        out_specs=(P("section", "ctx", None), P("section", "ctx", None), P("section", "ctx", None)),
        check_vma=False,
    )
```

profile of v0, /device:TPU:0, one launch (start us, length us, event | category | flops | bytes accessed | tf_op | source)
XLA Modules:
  0.0 288.2 jit_solution(15223730416516184084)
XLA Ops:
  4.4 23.1 %all-gather = s32[16,1,128]{2,1,0:T(1,128)S(1)} all-gather(s32[1,1,128]{2,1,0:T(1,128)} %bitcast.332), channel_id=1, replica_groups=mesh['section'=2,'ctx'=16] {'ctx'}, dimensions={0}, use_global_device_ids=true | all-gather | bytes 8704 | tf_op jit(solution)/shard_map/all_gather | solution.py:97
  31.3 244.2 %while.32 = (s32[]{:T(128)}, f32[128,7,128]{2,0,1:T(8,128)S(1)}, bf16[128,128]{1,0:T(8,128)(2,1)S(1)}, bf16[128,128]{1,0:T(8,128)(2,1)S(1)}, f32[128,128]{1,0:T(...) while((s32[]{:T(128)}, f32[128,7,128]{2,0,1:T(8,128)S(1)}, ...), condition=%wide.region_24.25_spmd.clone, body=%wide.region_3.24_spmd.clone.sunk | while | flops 296796448 | bytes 20107972 | solution.py:141
  31.7 4.4 %collective-permute-start.1 = (bf16[128,128]{1,0:T(8,128)(2,1)}, bf16[128,128]{1,0:T(8,128)(2,1)S(1)}, u32[]{:S(2)}, u32[]{:S(2)}) collective-permute-start(bf16[128,128]{1,0:T(8,128)(2,1)} %get-tuple-element.1157), channel_id=1, source_target_pairs={{1,0},{2,1},{3,2},{4,3},{5,4},{6,5},{7,6},{8,7},{9,8},{10,9},{11,1... | collective-permute-start | bytes 98312 | tf_op jit(solution)/shard_map/while/body/eval_jaxpr/ppermute | solution.py:10
  56.5 1.7 collective-permute-start.5
  58.7 4.1 %collective-permute-done.5 = f32[128,128]{1,0:T(8,128)S(1)} collective-permute-done((f32[128,128]{1,0:T(8,128)S(1)}, f32[128,128]{1,0:T(8,128)S(1)}, u32[]{:S(2)}, u32[]{:S(2)}) %collective-permute-start.5) | collective-permute-done | bytes 65568 | tf_op jit(solution)/shard_map/while/body/eval_jaxpr/ppermute | solution.py:10
  62.9 4.4 %collective-permute-start.1 = (bf16[128,128]{1,0:T(8,128)(2,1)}, bf16[128,128]{1,0:T(8,128)(2,1)S(1)}, u32[]{:S(2)}, u32[]{:S(2)}) collective-permute-start(bf16[128,128]{1,0:T(8,128)(2,1)} %get-tuple-element.1157), channel_id=1, source_target_pairs={{1,0},{2,1},{3,2},{4,3},{5,4},{6,5},{7,6},{8,7},{9,8},{10,9},{11,1... | collective-permute-start | bytes 98312 | tf_op jit(solution)/shard_map/while/body/eval_jaxpr/ppermute | solution.py:10
  89.1 4.1 %collective-permute-done.5 = f32[128,128]{1,0:T(8,128)S(1)} collective-permute-done((f32[128,128]{1,0:T(8,128)S(1)}, f32[128,128]{1,0:T(8,128)S(1)}, u32[]{:S(2)}, u32[]{:S(2)}) %collective-permute-start.5) | collective-permute-done | bytes 65568 | tf_op jit(solution)/shard_map/while/body/eval_jaxpr/ppermute | solution.py:10
  93.3 4.4 %collective-permute-start.1 = (bf16[128,128]{1,0:T(8,128)(2,1)}, bf16[128,128]{1,0:T(8,128)(2,1)S(1)}, u32[]{:S(2)}, u32[]{:S(2)}) collective-permute-start(bf16[128,128]{1,0:T(8,128)(2,1)} %get-tuple-element.1157), channel_id=1, source_target_pairs={{1,0},{2,1},{3,2},{4,3},{5,4},{6,5},{7,6},{8,7},{9,8},{10,9},{11,1... | collective-permute-start | bytes 98312 | tf_op jit(solution)/shard_map/while/body/eval_jaxpr/ppermute | solution.py:10
  119.5 4.1 %collective-permute-done.5 = f32[128,128]{1,0:T(8,128)S(1)} collective-permute-done((f32[128,128]{1,0:T(8,128)S(1)}, f32[128,128]{1,0:T(8,128)S(1)}, u32[]{:S(2)}, u32[]{:S(2)}) %collective-permute-start.5) | collective-permute-done | bytes 65568 | tf_op jit(solution)/shard_map/while/body/eval_jaxpr/ppermute | solution.py:10
  123.7 4.4 %collective-permute-start.1 = (bf16[128,128]{1,0:T(8,128)(2,1)}, bf16[128,128]{1,0:T(8,128)(2,1)S(1)}, u32[]{:S(2)}, u32[]{:S(2)}) collective-permute-start(bf16[128,128]{1,0:T(8,128)(2,1)} %get-tuple-element.1157), channel_id=1, source_target_pairs={{1,0},{2,1},{3,2},{4,3},{5,4},{6,5},{7,6},{8,7},{9,8},{10,9},{11,1... | collective-permute-start | bytes 98312 | tf_op jit(solution)/shard_map/while/body/eval_jaxpr/ppermute | solution.py:10
  147.6 1.7 collective-permute-start.5
  149.8 4.1 %collective-permute-done.5 = f32[128,128]{1,0:T(8,128)S(1)} collective-permute-done((f32[128,128]{1,0:T(8,128)S(1)}, f32[128,128]{1,0:T(8,128)S(1)}, u32[]{:S(2)}, u32[]{:S(2)}) %collective-permute-start.5) | collective-permute-done | bytes 65568 | tf_op jit(solution)/shard_map/while/body/eval_jaxpr/ppermute | solution.py:10
  154.0 4.4 %collective-permute-start.1 = (bf16[128,128]{1,0:T(8,128)(2,1)}, bf16[128,128]{1,0:T(8,128)(2,1)S(1)}, u32[]{:S(2)}, u32[]{:S(2)}) collective-permute-start(bf16[128,128]{1,0:T(8,128)(2,1)} %get-tuple-element.1157), channel_id=1, source_target_pairs={{1,0},{2,1},{3,2},{4,3},{5,4},{6,5},{7,6},{8,7},{9,8},{10,9},{11,1... | collective-permute-start | bytes 98312 | tf_op jit(solution)/shard_map/while/body/eval_jaxpr/ppermute | solution.py:10
  180.2 4.2 %collective-permute-done.5 = f32[128,128]{1,0:T(8,128)S(1)} collective-permute-done((f32[128,128]{1,0:T(8,128)S(1)}, f32[128,128]{1,0:T(8,128)S(1)}, u32[]{:S(2)}, u32[]{:S(2)}) %collective-permute-start.5) | collective-permute-done | bytes 65568 | tf_op jit(solution)/shard_map/while/body/eval_jaxpr/ppermute | solution.py:10
  184.4 4.4 %collective-permute-start.1 = (bf16[128,128]{1,0:T(8,128)(2,1)}, bf16[128,128]{1,0:T(8,128)(2,1)S(1)}, u32[]{:S(2)}, u32[]{:S(2)}) collective-permute-start(bf16[128,128]{1,0:T(8,128)(2,1)} %get-tuple-element.1157), channel_id=1, source_target_pairs={{1,0},{2,1},{3,2},{4,3},{5,4},{6,5},{7,6},{8,7},{9,8},{10,9},{11,1... | collective-permute-start | bytes 98312 | tf_op jit(solution)/shard_map/while/body/eval_jaxpr/ppermute | solution.py:10
  208.3 1.7 collective-permute-start.5
  210.6 4.1 %collective-permute-done.5 = f32[128,128]{1,0:T(8,128)S(1)} collective-permute-done((f32[128,128]{1,0:T(8,128)S(1)}, f32[128,128]{1,0:T(8,128)S(1)}, u32[]{:S(2)}, u32[]{:S(2)}) %collective-permute-start.5) | collective-permute-done | bytes 65568 | tf_op jit(solution)/shard_map/while/body/eval_jaxpr/ppermute | solution.py:10
  214.8 4.4 %collective-permute-start.1 = (bf16[128,128]{1,0:T(8,128)(2,1)}, bf16[128,128]{1,0:T(8,128)(2,1)S(1)}, u32[]{:S(2)}, u32[]{:S(2)}) collective-permute-start(bf16[128,128]{1,0:T(8,128)(2,1)} %get-tuple-element.1157), channel_id=1, source_target_pairs={{1,0},{2,1},{3,2},{4,3},{5,4},{6,5},{7,6},{8,7},{9,8},{10,9},{11,1... | collective-permute-start | bytes 98312 | tf_op jit(solution)/shard_map/while/body/eval_jaxpr/ppermute | solution.py:10
  238.7 1.7 collective-permute-start.5
  241.0 4.1 %collective-permute-done.5 = f32[128,128]{1,0:T(8,128)S(1)} collective-permute-done((f32[128,128]{1,0:T(8,128)S(1)}, f32[128,128]{1,0:T(8,128)S(1)}, u32[]{:S(2)}, u32[]{:S(2)}) %collective-permute-start.5) | collective-permute-done | bytes 65568 | tf_op jit(solution)/shard_map/while/body/eval_jaxpr/ppermute | solution.py:10
  245.2 4.4 %collective-permute-start.1 = (bf16[128,128]{1,0:T(8,128)(2,1)}, bf16[128,128]{1,0:T(8,128)(2,1)S(1)}, u32[]{:S(2)}, u32[]{:S(2)}) collective-permute-start(bf16[128,128]{1,0:T(8,128)(2,1)} %get-tuple-element.1157), channel_id=1, source_target_pairs={{1,0},{2,1},{3,2},{4,3},{5,4},{6,5},{7,6},{8,7},{9,8},{10,9},{11,1... | collective-permute-start | bytes 98312 | tf_op jit(solution)/shard_map/while/body/eval_jaxpr/ppermute | solution.py:10
  271.3 4.2 %collective-permute-done.5 = f32[128,128]{1,0:T(8,128)S(1)} collective-permute-done((f32[128,128]{1,0:T(8,128)S(1)}, f32[128,128]{1,0:T(8,128)S(1)}, u32[]{:S(2)}, u32[]{:S(2)}) %collective-permute-start.5) | collective-permute-done | bytes 65568 | tf_op jit(solution)/shard_map/while/body/eval_jaxpr/ppermute | solution.py:10
  277.4 3.0 %collective-permute-start.11 = (bf16[128,128]{1,0:T(8,128)(2,1)S(1)}, bf16[128,128]{1,0:T(8,128)(2,1)S(1)}, u32[]{:S(2)}, u32[]{:S(2)}) collective-permute-start(bf16[128,128]{1,0:T(8,128)(2,1)S(1)} %add_convert_fusion), channel_id=1, source_target_pairs={{8,0},{9,1},{10,2},{11,3},{12,4},{13,5},{14,6},{15,7},{0,8},{1,9},... | collective-permute-start | bytes 98312 | tf_op jit(solution)/shard_map/ppermute | solution.py:10
  284.3 1.9 collective-permute-done.12
  (758 shorter events, 142.5 us)
Async XLA Ops:
  31.3 26.9 %collective-permute-start.2 = (bf16[128,128]{1,0:T(8,128)(2,1)S(1)}, bf16[128,128]{1,0:T(8,128)(2,1)S(1)}, u32[]{:S(2)}, u32[]{:S(2)}) collective-permute-start(bf16[128,128]{1,0:T(8,128)(2,1)S(1)} %copy.120), channel_id=1, source_target_pairs={{15,0},{0,1},{1,2},{2,3},{3,4},{4,5},{5,6},{6,7},{7,8},{8,9},{9,10... | collective-permute-start | bytes 98312 | tf_op jit(solution)/shard_map/while/body/eval_jaxpr/ppermute | solution.py:10
  31.6 26.6 %collective-permute-start.3 = (bf16[128,128]{1,0:T(8,128)(2,1)S(1)}, bf16[128,128]{1,0:T(8,128)(2,1)S(1)}, u32[]{:S(2)}, u32[]{:S(2)}) collective-permute-start(bf16[128,128]{1,0:T(8,128)(2,1)S(1)} %copy.121), channel_id=1, source_target_pairs={{15,0},{0,1},{1,2},{2,3},{3,4},{4,5},{5,6},{6,7},{7,8},{8,9},{9,10... | collective-permute-start | bytes 98312 | tf_op jit(solution)/shard_map/while/body/eval_jaxpr/ppermute | solution.py:10
  36.3 21.9 %collective-permute-start.6 = (f32[128,128]{1,0:T(8,128)S(1)}, f32[128,128]{1,0:T(8,128)S(1)}, u32[]{:S(2)}, u32[]{:S(2)}) collective-permute-start(f32[128,128]{1,0:T(8,128)S(1)} %broadcast_select_fusion.4), channel_id=1, source_target_pairs={{1,0},{2,1},{3,2},{4,3},{5,4},{6,5},{7,6},{8,7},{9,8},{10,9},{11,1... | collective-permute-start | bytes 196616 | tf_op jit(solution)/shard_map/while/body/eval_jaxpr/ppermute | solution.py:10
  62.9 25.7 %collective-permute-start.2 = (bf16[128,128]{1,0:T(8,128)(2,1)S(1)}, bf16[128,128]{1,0:T(8,128)(2,1)S(1)}, u32[]{:S(2)}, u32[]{:S(2)}) collective-permute-start(bf16[128,128]{1,0:T(8,128)(2,1)S(1)} %copy.120), channel_id=1, source_target_pairs={{15,0},{0,1},{1,2},{2,3},{3,4},{4,5},{5,6},{6,7},{7,8},{8,9},{9,10... | collective-permute-start | bytes 98312 | tf_op jit(solution)/shard_map/while/body/eval_jaxpr/ppermute | solution.py:10
  62.9 25.7 %collective-permute-start.3 = (bf16[128,128]{1,0:T(8,128)(2,1)S(1)}, bf16[128,128]{1,0:T(8,128)(2,1)S(1)}, u32[]{:S(2)}, u32[]{:S(2)}) collective-permute-start(bf16[128,128]{1,0:T(8,128)(2,1)S(1)} %copy.121), channel_id=1, source_target_pairs={{15,0},{0,1},{1,2},{2,3},{3,4},{4,5},{5,6},{6,7},{7,8},{8,9},{9,10... | collective-permute-start | bytes 98312 | tf_op jit(solution)/shard_map/while/body/eval_jaxpr/ppermute | solution.py:10
  67.8 20.7 %collective-permute-start.6 = (f32[128,128]{1,0:T(8,128)S(1)}, f32[128,128]{1,0:T(8,128)S(1)}, u32[]{:S(2)}, u32[]{:S(2)}) collective-permute-start(f32[128,128]{1,0:T(8,128)S(1)} %broadcast_select_fusion.4), channel_id=1, source_target_pairs={{1,0},{2,1},{3,2},{4,3},{5,4},{6,5},{7,6},{8,7},{9,8},{10,9},{11,1... | collective-permute-start | bytes 196616 | tf_op jit(solution)/shard_map/while/body/eval_jaxpr/ppermute | solution.py:10
  93.2 25.7 %collective-permute-start.2 = (bf16[128,128]{1,0:T(8,128)(2,1)S(1)}, bf16[128,128]{1,0:T(8,128)(2,1)S(1)}, u32[]{:S(2)}, u32[]{:S(2)}) collective-permute-start(bf16[128,128]{1,0:T(8,128)(2,1)S(1)} %copy.120), channel_id=1, source_target_pairs={{15,0},{0,1},{1,2},{2,3},{3,4},{4,5},{5,6},{6,7},{7,8},{8,9},{9,10... | collective-permute-start | bytes 98312 | tf_op jit(solution)/shard_map/while/body/eval_jaxpr/ppermute | solution.py:10
  93.2 25.7 %collective-permute-start.3 = (bf16[128,128]{1,0:T(8,128)(2,1)S(1)}, bf16[128,128]{1,0:T(8,128)(2,1)S(1)}, u32[]{:S(2)}, u32[]{:S(2)}) collective-permute-start(bf16[128,128]{1,0:T(8,128)(2,1)S(1)} %copy.121), channel_id=1, source_target_pairs={{15,0},{0,1},{1,2},{2,3},{3,4},{4,5},{5,6},{6,7},{7,8},{8,9},{9,10... | collective-permute-start | bytes 98312 | tf_op jit(solution)/shard_map/while/body/eval_jaxpr/ppermute | solution.py:10
  98.2 20.7 %collective-permute-start.6 = (f32[128,128]{1,0:T(8,128)S(1)}, f32[128,128]{1,0:T(8,128)S(1)}, u32[]{:S(2)}, u32[]{:S(2)}) collective-permute-start(f32[128,128]{1,0:T(8,128)S(1)} %broadcast_select_fusion.4), channel_id=1, source_target_pairs={{1,0},{2,1},{3,2},{4,3},{5,4},{6,5},{7,6},{8,7},{9,8},{10,9},{11,1... | collective-permute-start | bytes 196616 | tf_op jit(solution)/shard_map/while/body/eval_jaxpr/ppermute | solution.py:10
  123.6 25.7 %collective-permute-start.2 = (bf16[128,128]{1,0:T(8,128)(2,1)S(1)}, bf16[128,128]{1,0:T(8,128)(2,1)S(1)}, u32[]{:S(2)}, u32[]{:S(2)}) collective-permute-start(bf16[128,128]{1,0:T(8,128)(2,1)S(1)} %copy.120), channel_id=1, source_target_pairs={{15,0},{0,1},{1,2},{2,3},{3,4},{4,5},{5,6},{6,7},{7,8},{8,9},{9,10... | collective-permute-start | bytes 98312 | tf_op jit(solution)/shard_map/while/body/eval_jaxpr/ppermute | solution.py:10
  123.6 25.7 %collective-permute-start.3 = (bf16[128,128]{1,0:T(8,128)(2,1)S(1)}, bf16[128,128]{1,0:T(8,128)(2,1)S(1)}, u32[]{:S(2)}, u32[]{:S(2)}) collective-permute-start(bf16[128,128]{1,0:T(8,128)(2,1)S(1)} %copy.121), channel_id=1, source_target_pairs={{15,0},{0,1},{1,2},{2,3},{3,4},{4,5},{5,6},{6,7},{7,8},{8,9},{9,10... | collective-permute-start | bytes 98312 | tf_op jit(solution)/shard_map/while/body/eval_jaxpr/ppermute | solution.py:10
  128.6 20.7 %collective-permute-start.6 = (f32[128,128]{1,0:T(8,128)S(1)}, f32[128,128]{1,0:T(8,128)S(1)}, u32[]{:S(2)}, u32[]{:S(2)}) collective-permute-start(f32[128,128]{1,0:T(8,128)S(1)} %broadcast_select_fusion.4), channel_id=1, source_target_pairs={{1,0},{2,1},{3,2},{4,3},{5,4},{6,5},{7,6},{8,7},{9,8},{10,9},{11,1... | collective-permute-start | bytes 196616 | tf_op jit(solution)/shard_map/while/body/eval_jaxpr/ppermute | solution.py:10
  154.0 25.7 %collective-permute-start.2 = (bf16[128,128]{1,0:T(8,128)(2,1)S(1)}, bf16[128,128]{1,0:T(8,128)(2,1)S(1)}, u32[]{:S(2)}, u32[]{:S(2)}) collective-permute-start(bf16[128,128]{1,0:T(8,128)(2,1)S(1)} %copy.120), channel_id=1, source_target_pairs={{15,0},{0,1},{1,2},{2,3},{3,4},{4,5},{5,6},{6,7},{7,8},{8,9},{9,10... | collective-permute-start | bytes 98312 | tf_op jit(solution)/shard_map/while/body/eval_jaxpr/ppermute | solution.py:10
  154.0 25.7 %collective-permute-start.3 = (bf16[128,128]{1,0:T(8,128)(2,1)S(1)}, bf16[128,128]{1,0:T(8,128)(2,1)S(1)}, u32[]{:S(2)}, u32[]{:S(2)}) collective-permute-start(bf16[128,128]{1,0:T(8,128)(2,1)S(1)} %copy.121), channel_id=1, source_target_pairs={{15,0},{0,1},{1,2},{2,3},{3,4},{4,5},{5,6},{6,7},{7,8},{8,9},{9,10... | collective-permute-start | bytes 98312 | tf_op jit(solution)/shard_map/while/body/eval_jaxpr/ppermute | solution.py:10
  158.9 20.7 %collective-permute-start.6 = (f32[128,128]{1,0:T(8,128)S(1)}, f32[128,128]{1,0:T(8,128)S(1)}, u32[]{:S(2)}, u32[]{:S(2)}) collective-permute-start(f32[128,128]{1,0:T(8,128)S(1)} %broadcast_select_fusion.4), channel_id=1, source_target_pairs={{1,0},{2,1},{3,2},{4,3},{5,4},{6,5},{7,6},{8,7},{9,8},{10,9},{11,1... | collective-permute-start | bytes 196616 | tf_op jit(solution)/shard_map/while/body/eval_jaxpr/ppermute | solution.py:10
  184.4 25.7 %collective-permute-start.2 = (bf16[128,128]{1,0:T(8,128)(2,1)S(1)}, bf16[128,128]{1,0:T(8,128)(2,1)S(1)}, u32[]{:S(2)}, u32[]{:S(2)}) collective-permute-start(bf16[128,128]{1,0:T(8,128)(2,1)S(1)} %copy.120), channel_id=1, source_target_pairs={{15,0},{0,1},{1,2},{2,3},{3,4},{4,5},{5,6},{6,7},{7,8},{8,9},{9,10... | collective-permute-start | bytes 98312 | tf_op jit(solution)/shard_map/while/body/eval_jaxpr/ppermute | solution.py:10
  184.4 25.7 %collective-permute-start.3 = (bf16[128,128]{1,0:T(8,128)(2,1)S(1)}, bf16[128,128]{1,0:T(8,128)(2,1)S(1)}, u32[]{:S(2)}, u32[]{:S(2)}) collective-permute-start(bf16[128,128]{1,0:T(8,128)(2,1)S(1)} %copy.121), channel_id=1, source_target_pairs={{15,0},{0,1},{1,2},{2,3},{3,4},{4,5},{5,6},{6,7},{7,8},{8,9},{9,10... | collective-permute-start | bytes 98312 | tf_op jit(solution)/shard_map/while/body/eval_jaxpr/ppermute | solution.py:10
  189.3 20.7 %collective-permute-start.6 = (f32[128,128]{1,0:T(8,128)S(1)}, f32[128,128]{1,0:T(8,128)S(1)}, u32[]{:S(2)}, u32[]{:S(2)}) collective-permute-start(f32[128,128]{1,0:T(8,128)S(1)} %broadcast_select_fusion.4), channel_id=1, source_target_pairs={{1,0},{2,1},{3,2},{4,3},{5,4},{6,5},{7,6},{8,7},{9,8},{10,9},{11,1... | collective-permute-start | bytes 196616 | tf_op jit(solution)/shard_map/while/body/eval_jaxpr/ppermute | solution.py:10
  214.7 25.7 %collective-permute-start.2 = (bf16[128,128]{1,0:T(8,128)(2,1)S(1)}, bf16[128,128]{1,0:T(8,128)(2,1)S(1)}, u32[]{:S(2)}, u32[]{:S(2)}) collective-permute-start(bf16[128,128]{1,0:T(8,128)(2,1)S(1)} %copy.120), channel_id=1, source_target_pairs={{15,0},{0,1},{1,2},{2,3},{3,4},{4,5},{5,6},{6,7},{7,8},{8,9},{9,10... | collective-permute-start | bytes 98312 | tf_op jit(solution)/shard_map/while/body/eval_jaxpr/ppermute | solution.py:10
  214.7 25.7 %collective-permute-start.3 = (bf16[128,128]{1,0:T(8,128)(2,1)S(1)}, bf16[128,128]{1,0:T(8,128)(2,1)S(1)}, u32[]{:S(2)}, u32[]{:S(2)}) collective-permute-start(bf16[128,128]{1,0:T(8,128)(2,1)S(1)} %copy.121), channel_id=1, source_target_pairs={{15,0},{0,1},{1,2},{2,3},{3,4},{4,5},{5,6},{6,7},{7,8},{8,9},{9,10... | collective-permute-start | bytes 98312 | tf_op jit(solution)/shard_map/while/body/eval_jaxpr/ppermute | solution.py:10
  219.7 20.7 %collective-permute-start.6 = (f32[128,128]{1,0:T(8,128)S(1)}, f32[128,128]{1,0:T(8,128)S(1)}, u32[]{:S(2)}, u32[]{:S(2)}) collective-permute-start(f32[128,128]{1,0:T(8,128)S(1)} %broadcast_select_fusion.4), channel_id=1, source_target_pairs={{1,0},{2,1},{3,2},{4,3},{5,4},{6,5},{7,6},{8,7},{9,8},{10,9},{11,1... | collective-permute-start | bytes 196616 | tf_op jit(solution)/shard_map/while/body/eval_jaxpr/ppermute | solution.py:10
  245.1 25.7 %collective-permute-start.2 = (bf16[128,128]{1,0:T(8,128)(2,1)S(1)}, bf16[128,128]{1,0:T(8,128)(2,1)S(1)}, u32[]{:S(2)}, u32[]{:S(2)}) collective-permute-start(bf16[128,128]{1,0:T(8,128)(2,1)S(1)} %copy.120), channel_id=1, source_target_pairs={{15,0},{0,1},{1,2},{2,3},{3,4},{4,5},{5,6},{6,7},{7,8},{8,9},{9,10... | collective-permute-start | bytes 98312 | tf_op jit(solution)/shard_map/while/body/eval_jaxpr/ppermute | solution.py:10
  245.1 25.7 %collective-permute-start.3 = (bf16[128,128]{1,0:T(8,128)(2,1)S(1)}, bf16[128,128]{1,0:T(8,128)(2,1)S(1)}, u32[]{:S(2)}, u32[]{:S(2)}) collective-permute-start(bf16[128,128]{1,0:T(8,128)(2,1)S(1)} %copy.121), channel_id=1, source_target_pairs={{15,0},{0,1},{1,2},{2,3},{3,4},{4,5},{5,6},{6,7},{7,8},{8,9},{9,10... | collective-permute-start | bytes 98312 | tf_op jit(solution)/shard_map/while/body/eval_jaxpr/ppermute | solution.py:10
  250.1 20.7 %collective-permute-start.6 = (f32[128,128]{1,0:T(8,128)S(1)}, f32[128,128]{1,0:T(8,128)S(1)}, u32[]{:S(2)}, u32[]{:S(2)}) collective-permute-start(f32[128,128]{1,0:T(8,128)S(1)} %broadcast_select_fusion.4), channel_id=1, source_target_pairs={{1,0},{2,1},{3,2},{4,3},{5,4},{6,5},{7,6},{8,7},{9,8},{10,9},{11,1... | collective-permute-start | bytes 196616 | tf_op jit(solution)/shard_map/while/body/eval_jaxpr/ppermute | solution.py:10
  (49 other events, 475.9 us)
where the time goes:
time: 290 us; the launch traced here: 288 us
  loops' own time  84.7 us (29%)
  starting transfers between devices  64.6 us (22%)
  waiting for transfers between devices  41.2 us (14%)
  matrix products  37.2 us (13%)
  blocking collectives  23.1 us (8%)
  other arithmetic  20.5 us (7%)
  local copies, waits for them, and re-layouts  16.1 us (6%)
    another operation x1, loops' own time, shards(): lax.fori_loop(0, half_cycle, two_step, start_state)  82.3 us
    ppermute x69, starting transfers between devices, from_behind(): return lax.ppermute(block, axis, route)  64.6 us
    ppermute x69, waiting for transfers between devices, from_behind(): return lax.ppermute(block, axis, route)  41.2 us
    all_gather x1, blocking collectives, shards(): all_positions = lax.all_gather(positions, 'ctx', axis=0, tiled=True)  23.1 us
    reduce_min x16, other arithmetic, block_terms(): masked_out = jnp.min(key_pos[key_slice]) > jnp.max(query_pos[query_slice])  12.3 us
    dot_general x33, matrix products, tile_terms(): jnp.einsum('ihd,jd->hij', query_part, key_part, preferred_element_type=jn...  8.23 us
    dot_general x33, matrix products, tile_terms(): jnp.einsum('ihd,jd->hij', grad_part, value_part, preferred_element_type=j...  8.05 us
    unnamed x21, local copies, waits for them, and re-layouts  7.95 us
  transfers between devices with their start and end apart: 69, of which 19 were waited for; matrix products, arithmetic and copies ran while one was open for 22% of the time, Pallas kernels for 0%

commit v1 on v0

v1 whole, which is shorter than its diff:
```python
import functools
import math

import jax
import jax.numpy as jnp
from jax import lax
from jax.experimental import pallas as pl
from jax.experimental.pallas import tpu as pltpu
from jax.sharding import PartitionSpec as P

MESH = pl.DeviceIdType.MESH
LOG2E = 1.0 / math.log(2.0)
NT = (((1,), (1,)), ((), ()))
NN = (((1,), (0,)), ((), ()))
TN = (((0,), (0,)), ((), ()))


def dot(a, b, dims):
    return lax.dot_general(a, b, dims, preferred_element_type=jnp.float32)


def grid_of(ctx):
    chips = ctx // 2
    across = 1 << ((chips.bit_length() - 1) // 2)
    return chips // across, across


def kernel(
    sections, zs, xs, group,
    q_ref, k_ref, v_ref, o_ref, g_ref, norm_ref, pos_ref,
    dq_out, dk_out, dv_out,
    kv, qs, gs, rows_norm, rows_dot, dq_sum, part, part_low, core_in, x_out, x_in, z_out, z_in,
    kv_done, kv_in, dq_low,
    gz_send, gz_recv, gx_send, gx_recv, gc_send, gc_recv,
    rc_send, rc_recv, rx_send, rx_recv, rz_send, rz_recv, y_send, y_recv,
):
    rows, head = k_ref.shape
    half = rows // 2
    runs = zs * xs * 2 * 2
    scale = head ** -0.5
    s = lax.axis_index("section")
    me = lax.axis_index("ctx")
    c = lax.rem(me, 2)
    chip = lax.div(me, 2)
    x = lax.rem(chip, xs)
    z = lax.div(chip, xs)

    def shift(value, by, size):
        return lax.rem(value + (by + size), size)

    def device(zz, xx, cc):
        return (s, (zz * xs + xx) * 2 + cc)

    def z_peer(d):
        return device(shift(z, d, zs), x, c)

    def x_peer(d):
        return device(z, shift(x, d, xs), c)

    core_peer = device(z, x, 1 - c)
    before = (shift(s, -1, sections), me)
    after = (shift(s, 1, sections), me)

    def send(src, dst, send_sem, recv_sem, to):
        copy = pltpu.make_async_remote_copy(
            src_ref=src, dst_ref=dst, send_sem=send_sem, recv_sem=recv_sem,
            device_id=to, device_id_type=MESH,
        )
        return copy

    kv[chip, c, 0:rows] = k_ref[...]
    kv[chip, c, rows:2 * rows] = v_ref[...]
    run = lax.shift_right_logical(pos_ref[0:1, 0:1], half.bit_length() - 1).astype(jnp.float32)
    kv[chip, c, 2 * rows:] = jnp.broadcast_to(run, (16, head)).astype(jnp.bfloat16)

    barrier = pltpu.get_barrier_semaphore()
    peers = [z_peer(d) for d in range(1, zs)] + [x_peer(d) for d in range(1, xs)]
    peers += [core_peer, before]
    if sections > 2:
        peers.append(after)
    for peer in peers:
        pl.semaphore_signal(barrier, inc=1, device_id=peer, device_id_type=MESH)
    pl.semaphore_wait(barrier, len(peers))

    started = []

    def begin(copy):
        copy.start()
        started.append(copy)
        return copy

    def chip_at(dz, dx):
        return shift(z, -dz, zs) * xs + shift(x, -dx, xs)

    z_copies = {}
    for dz in range(1, zs):
        z_copies[dz] = begin(send(kv.at[chip, c], kv.at[chip, c], gz_send.at[dz], gz_recv.at[dz], z_peer(dz)))
    x_copies, c_copies = {}, {}

    def forward_x(dz):
        t = chip_at(dz, 0)
        for dx in range(1, xs):
            x_copies[dz, dx] = begin(send(
                kv.at[t, c], kv.at[t, c], gx_send.at[dz, dx], gx_recv.at[dz, dx], x_peer(dx)))

    def forward_c(dz, dx):
        t = chip_at(dz, dx)
        c_copies[dz, dx] = begin(send(
            kv.at[t, c], kv.at[t, c], gc_send.at[dz, dx], gc_recv.at[dz, dx], core_peer))

    forward_x(0)
    forward_c(0, 0)

    ones = jnp.ones((8, head), jnp.bfloat16)
    for h in range(group):
        cols = slice(h * head, (h + 1) * head)
        there = slice(h * rows, (h + 1) * rows)
        qs[there] = q_ref[:, cols]
        grad = g_ref[:, cols]
        gs[there] = grad
        prod = grad.astype(jnp.float32) * o_ref[:, cols].astype(jnp.float32)
        high = prod.astype(jnp.bfloat16)
        low = (prod - high.astype(jnp.float32)).astype(jnp.bfloat16)
        total = dot(ones, high, NT) + dot(ones, low, NT)
        rows_dot[:, there] = total
        rows_norm[:, there] = jnp.broadcast_to(norm_ref[h:h + 1, :] * LOG2E, (8, rows))
    dq_sum[...] = jnp.zeros_like(dq_sum)

    for dz in range(1, zs + 1):
        if dz < zs:
            z_copies[dz].wait_recv()
            forward_x(dz)
            forward_c(dz, 0)
        for dx in range(1, xs):
            x_copies[dz - 1, dx].wait_recv()
            forward_c(dz - 1, dx)
    for copy in c_copies.values():
        copy.wait_recv()

    query_pos = pos_ref[...].astype(jnp.float32)
    row_at = lax.broadcasted_iota(jnp.int32, (half, rows), 0).astype(jnp.float32)
    chunks = [(a, min(a + 2, group)) for a in range(0, group, 2)]

    def blocks(t, _):
        keys = kv[t, :, 0:rows].reshape(2 * rows, head)
        values = kv[t, :, rows:2 * rows].reshape(2 * rows, head)
        bias = []
        for core in range(2):
            first = kv[t, core, 2 * rows:].astype(jnp.float32)[0:1, :]
            low_pos = first * half + row_at
            high_pos = (runs - 1 - first) * half + row_at
            for key_pos in (low_pos, high_pos):
                bias.append(jnp.where(key_pos <= query_pos, 0.0, -1e30))
        bias = jnp.concatenate(bias, axis=0)
        dk = jnp.zeros((2 * rows, head), jnp.float32)
        dv = jnp.zeros((2 * rows, head), jnp.float32)
        for a, b in chunks:
            there = slice(a * rows, b * rows)
            query, grad = qs[there], gs[there]
            scores = dot(keys, query, NT)
            wide = jnp.concatenate([bias] * (b - a), axis=1)
            probs = jnp.exp2((scores * (scale * LOG2E) - rows_norm[0:1, there]) + wide)
            dprobs = dot(values, grad, NT)
            dscores = (probs * (dprobs - rows_dot[0:1, there])).astype(jnp.bfloat16)
            dv = dv + dot(probs.astype(jnp.bfloat16), grad, NN)
            dk = dk + dot(dscores, query, NN)
            dq_sum[there] += dot(dscores, keys, TN)
        dk = dk * scale
        for core in range(2):
            these = slice(core * rows, (core + 1) * rows)
            part[t, core, 0:rows] = dk[these]
            part[t, core, rows:] = dv[these]
            part_low[t, core, 0:rows] = dk[these].astype(jnp.bfloat16)
            part_low[t, core, rows:] = dv[these].astype(jnp.bfloat16)
        return 0

    lax.fori_loop(0, zs * xs, blocks, 0)

    core_copies = {}
    order = [zs - 1 - i for i in range(zs)]
    for dz in order:
        for dx in range(xs):
            t = chip_at(-dz, -dx)
            core_copies[dz, dx] = begin(send(
                part_low.at[t, 1 - c], core_in.at[t], rc_send.at[dz, dx], rc_recv.at[dz, dx], core_peer))
    for h in range(group):
        dq_low[:, h * head:(h + 1) * head] = (
            dq_sum[h * rows:(h + 1) * rows] * scale).astype(jnp.bfloat16)
    dq_copy = begin(send(dq_low, dq_out, y_send.at[0], y_recv.at[0], before))

    rx_copies = {}
    for dz in order:
        for dx in range(xs - 1, -1, -1):
            core_copies[dz, dx].wait_recv()
            t = chip_at(-dz, -dx)
            total = part[t, c] + core_in[t].astype(jnp.float32)
            if dx:
                x_out[dz, dx] = total.astype(jnp.bfloat16)
                rx_copies[dz, dx] = begin(send(
                    x_out.at[dz, dx], x_in.at[dz, dx], rx_send.at[dz, dx], rx_recv.at[dz, dx], x_peer(dx)))
            else:
                part[t, c] = total
    rz_copies = {}
    for dz in order:
        total = part[chip_at(-dz, 0), c]
        for dx in range(1, xs):
            rx_copies[dz, dx].wait_recv()
            total = total + x_in[dz, dx].astype(jnp.float32)
        if dz:
            z_out[dz] = total.astype(jnp.bfloat16)
            rz_copies[dz] = begin(send(
                z_out.at[dz], z_in.at[dz], rz_send.at[dz], rz_recv.at[dz], z_peer(dz)))
    for dz in range(1, zs):
        rz_copies[dz].wait_recv()
        total = total + z_in[dz].astype(jnp.float32)
    kv_done[...] = total.astype(jnp.bfloat16)
    kv_copy = begin(send(kv_done, kv_in, y_send.at[1], y_recv.at[1], before))
    kv_copy.wait_recv()
    dk_out[...] = kv_in[0:rows]
    dv_out[...] = kv_in[rows:]
    dq_copy.wait_recv()
    for copy in started:
        copy.wait_send()


def solution(mesh):
    sections = mesh.shape["section"]
    zs, xs = grid_of(mesh.shape["ctx"])

    def shards(query_rows, key_rows, value_rows, attn_output, grad_output, log_normalizer, positions):
        rows, head = key_rows.shape[1:]
        wide = query_rows.shape[2]
        group = wide // head
        chips = zs * xs
        bf16, f32 = jnp.bfloat16, jnp.float32
        dma = pltpu.SemaphoreType.DMA
        vmem = pl.BlockSpec(memory_space=pltpu.VMEM)
        dq, dk, dv = pl.pallas_call(
            functools.partial(kernel, sections, zs, xs, group),
            out_shape=(
                jax.ShapeDtypeStruct((rows, wide), bf16),
                jax.ShapeDtypeStruct((rows, head), bf16),
                jax.ShapeDtypeStruct((rows, head), bf16),
            ),
            in_specs=[vmem] * 7,
            out_specs=(vmem,) * 3,
            scratch_shapes=[
                pltpu.VMEM((chips, 2, 2 * rows + 16, head), bf16),
                pltpu.VMEM((group * rows, head), bf16),
                pltpu.VMEM((group * rows, head), bf16),
                pltpu.VMEM((8, group * rows), f32),
                pltpu.VMEM((8, group * rows), f32),
                pltpu.VMEM((group * rows, head), f32),
                pltpu.VMEM((chips, 2, 2 * rows, head), f32),
                pltpu.VMEM((chips, 2, 2 * rows, head), bf16),
                pltpu.VMEM((chips, 2 * rows, head), bf16),
                pltpu.VMEM((zs, xs, 2 * rows, head), bf16),
                pltpu.VMEM((zs, xs, 2 * rows, head), bf16),
                pltpu.VMEM((zs, 2 * rows, head), bf16),
                pltpu.VMEM((zs, 2 * rows, head), bf16),
                pltpu.VMEM((2 * rows, head), bf16),
                pltpu.VMEM((2 * rows, head), bf16),
                pltpu.VMEM((rows, wide), bf16),
                dma((zs,)), dma((zs,)),
                dma((zs, xs)), dma((zs, xs)),
                dma((zs, xs)), dma((zs, xs)),
                dma((zs, xs)), dma((zs, xs)),
                dma((zs, xs)), dma((zs, xs)),
                dma((zs,)), dma((zs,)),
                dma((2,)), dma((2,)),
            ],
            compiler_params=pltpu.CompilerParams(
                collective_id=0, has_side_effects=True, vmem_limit_bytes=48 * 1024 * 1024
            ),
        )(
            query_rows[0], key_rows[0], value_rows[0], attn_output[0], grad_output[0],
            log_normalizer[0], positions.reshape(1, rows),
        )
        return dq[None], dk[None], dv[None]

    return jax.shard_map(
        shards,
        mesh=mesh,
        in_specs=(
            P("section", "ctx", None),
            P("section", "ctx", None),
            P("section", "ctx", None),
            P("section", "ctx", None),
            P("section", "ctx", None),
            P("section", None, "ctx"),
            P("ctx"),
        ),
        out_specs=(P("section", "ctx", None),) * 3,
        check_vma=False,
    )
```

time: 290 us -> 52.2 us (0.18)
  loops' own time: 84.7 us -> 0 us
  starting transfers between devices: 64.6 us -> 0 us
  Pallas kernels: 0 us -> 43.6 us
  waiting for transfers between devices: 41.2 us -> 0 us
  matrix products: 37.2 us -> 0 us
  blocking collectives: 23.1 us -> 0 us
  other arithmetic: 20.5 us -> 0 us
  local copies, waits for them, and re-layouts: 16.1 us -> 7.58 us
    another operation x65 -> x0, loops' own time: 84.7 us -> none  [the longest x1 82.3 us: shards(): lax.fori_loop(0, half_cycle, two_step, start_state)]
    ppermute x69 -> x0, starting transfers between devices: 64.6 us -> none  [from_behind(): return lax.ppermute(block, axis, route)]
    pallas_call x0 -> x1, Pallas kernels: none -> 43.6 us  [shards(): pl.pallas_call(functools.partial(kernel, sections, zs, xs, group), out_sh...]
    ppermute x69 -> x0, waiting for transfers between devices: 41.2 us -> none  [from_behind(): return lax.ppermute(block, axis, route)]
    dot_general x165 -> x0, matrix products: 37.2 us -> none  [the longest x33 8.23 us: tile_terms(): jnp.einsum('ihd,jd->hij', query_part, key_part, preferred_element_type=jn...]
    all_gather x1 -> x0, blocking collectives: 23.1 us -> none  [shards(): all_positions = lax.all_gather(positions, 'ctx', axis=0, tiled=True)]
    reduce_min x16 -> x0, other arithmetic: 12.3 us -> none  [block_terms(): masked_out = jnp.min(key_pos[key_slice]) > jnp.max(query_pos[query_slice])]
    while x33 -> x0, local copies, waits for them, and re-layouts: 5.18 us -> none
  transfers between devices with their start and end apart: 69 -> 0, of which waited for: 19 -> 0; matrix products, arithmetic and copies ran while one was open for 22% -> 0% of each run, Pallas kernels for 0% -> 0%
where the time goes in v1:
time: 52.2 us; the launch traced here: 51.8 us
  Pallas kernels  43.6 us (84%)
  local copies, waits for them, and re-layouts  7.58 us (15%)
  between operations  0.65 us (1%)
    pallas_call x1, Pallas kernels, shards(): pl.pallas_call(functools.partial(kernel, sections, zs, xs, group), out_sh...  43.6 us
    unnamed x18, local copies, waits for them, and re-layouts  7.58 us

profile of v1, /device:TPU:0, one launch (start us, length us, event | category | flops | bytes accessed | tf_op | source)
XLA Modules:
  0.0 51.8 jit_solution(15763739529311005508)
XLA Ops:
  0.6 0.0 copy-start.6
  0.6 0.7 %copy-done.6 = f32[1,7,128]{2,0,1:T(1,128)S(1)} copy-done((f32[1,7,128]{2,0,1:T(1,128)S(1)}, f32[1,7,128]{2,0,1:T(1,128)}, u32[]{:S(2)}) %copy-start.6) | copy-done | bytes 3608
  1.3 0.0 copy-start.5
  1.3 0.7 %copy-done.5 = s32[128]{0:T(128)S(1)} copy-done((s32[128]{0:T(128)S(1)}, s32[128]{0:T(128)}, u32[]{:S(2)}) %copy-start.5) | copy-done | bytes 536
  2.0 0.0 copy-start
  2.0 0.9 %copy-done = bf16[1,128,896]{2,1,0:T(8,128)(2,1)S(1)} copy-done((bf16[1,128,896]{2,1,0:T(8,128)(2,1)S(1)}, bf16[1,128,896]{2,1,0:T(8,128)(2,1)}, u32[]{:S(2)}) %copy-start) | copy-done | bytes 229400
  2.9 0.0 copy-start.1
  2.9 0.9 %copy-done.1 = bf16[1,128,896]{2,1,0:T(8,128)(2,1)S(1)} copy-done((bf16[1,128,896]{2,1,0:T(8,128)(2,1)S(1)}, bf16[1,128,896]{2,1,0:T(8,128)(2,1)}, u32[]{:S(2)}) %copy-start.1) | copy-done | bytes 229400
  3.9 0.0 copy-start.2
  3.9 0.9 %copy-done.2 = bf16[1,128,896]{2,1,0:T(8,128)(2,1)S(1)} copy-done((bf16[1,128,896]{2,1,0:T(8,128)(2,1)S(1)}, bf16[1,128,896]{2,1,0:T(8,128)(2,1)}, u32[]{:S(2)}) %copy-start.2) | copy-done | bytes 229400
  4.8 0.0 copy-start.3
  4.8 0.8 %copy-done.3 = bf16[1,128,128]{2,1,0:T(8,128)(2,1)S(1)} copy-done((bf16[1,128,128]{2,1,0:T(8,128)(2,1)S(1)}, bf16[1,128,128]{2,1,0:T(8,128)(2,1)}, u32[]{:S(2)}) %copy-start.3) | copy-done | bytes 32792
  5.5 0.0 copy-start.4
  5.6 0.8 %copy-done.4 = bf16[1,128,128]{2,1,0:T(8,128)(2,1)S(1)} copy-done((bf16[1,128,128]{2,1,0:T(8,128)(2,1)S(1)}, bf16[1,128,128]{2,1,0:T(8,128)(2,1)}, u32[]{:S(2)}) %copy-start.4) | copy-done | bytes 32792
  6.3 43.6 %shard_map.94 = (bf16[128,896]{1,0:T(8,128)(2,1)S(1)}, bf16[128,128]{1,0:T(8,128)(2,1)S(1)}, bf16[128,128]{1,0:T(8,128)(2,1)S(1)}) custom-call(bf16[128,896]{1,0:T(8,128)(2,1)S(1)} %bitcast.13, bf16[128,128]{1,0:T(8,128)(2,1)S(1)} %bitcast.18, bf16[128,128]{1,0:T(8,128)(2,1)S(1)} %bitcast.19, bf16[128,896]{1,0:T(8,128)(2,1)S(1)} %bitcast.14, ...), custom_call_target="tpu_custom_call" | custom-call | tf_op jit(solution)/shard_map/pallas_call | solution.py:238
  49.9 0.7 %copy.16 = bf16[1,128,896]{2,1,0:T(8,128)(2,1)} copy(bf16[1,128,896]{2,1,0:T(8,128)(2,1)S(1)} %bitcast.12) | data formatting | bytes 458752
  50.6 0.6 %copy.17 = bf16[1,128,128]{2,1,0:T(8,128)(2,1)} copy(bf16[1,128,128]{2,1,0:T(8,128)(2,1)S(1)} %bitcast.17) | data formatting | bytes 65536
  51.2 0.6 %copy.18 = bf16[1,128,128]{2,1,0:T(8,128)(2,1)} copy(bf16[1,128,128]{2,1,0:T(8,128)(2,1)S(1)} %bitcast.16) | data formatting | bytes 65536
  (1 shorter events, 0.0 us)
Async XLA Ops:
  0.6 0.7 %copy-start.6 = (f32[1,7,128]{2,0,1:T(1,128)S(1)}, f32[1,7,128]{2,0,1:T(1,128)}, u32[]{:S(2)}) copy-start(f32[1,7,128]{2,0,1:T(1,128)} %param.12) | copy-start | bytes 10756
  1.3 0.7 %copy-start.5 = (s32[128]{0:T(128)S(1)}, s32[128]{0:T(128)}, u32[]{:S(2)}) copy-start(s32[128]{0:T(128)} %param.13) | copy-start | bytes 1540
  2.0 0.9 %copy-start = (bf16[1,128,896]{2,1,0:T(8,128)(2,1)S(1)}, bf16[1,128,896]{2,1,0:T(8,128)(2,1)}, u32[]{:S(2)}) copy-start(bf16[1,128,896]{2,1,0:T(8,128)(2,1)} %param.7) | copy-start | bytes 688132
  2.9 0.9 %copy-start.1 = (bf16[1,128,896]{2,1,0:T(8,128)(2,1)S(1)}, bf16[1,128,896]{2,1,0:T(8,128)(2,1)}, u32[]{:S(2)}) copy-start(bf16[1,128,896]{2,1,0:T(8,128)(2,1)} %param.10) | copy-start | bytes 688132
  3.9 0.9 %copy-start.2 = (bf16[1,128,896]{2,1,0:T(8,128)(2,1)S(1)}, bf16[1,128,896]{2,1,0:T(8,128)(2,1)}, u32[]{:S(2)}) copy-start(bf16[1,128,896]{2,1,0:T(8,128)(2,1)} %param.11) | copy-start | bytes 688132
  4.8 0.8 %copy-start.3 = (bf16[1,128,128]{2,1,0:T(8,128)(2,1)S(1)}, bf16[1,128,128]{2,1,0:T(8,128)(2,1)}, u32[]{:S(2)}) copy-start(bf16[1,128,128]{2,1,0:T(8,128)(2,1)} %param.8) | copy-start | bytes 98308
  5.5 0.8 %copy-start.4 = (bf16[1,128,128]{2,1,0:T(8,128)(2,1)S(1)}, bf16[1,128,128]{2,1,0:T(8,128)(2,1)}, u32[]{:S(2)}) copy-start(bf16[1,128,128]{2,1,0:T(8,128)(2,1)} %param.9) | copy-start | bytes 98308

commit v2 on v1

--- a/solution.py
+++ b/solution.py
@@ -27,16 +27,17 @@
 
 def kernel(
     sections, zs, xs, group,
-    q_ref, k_ref, v_ref, o_ref, g_ref, norm_ref, pos_ref,
+    q_hbm, k_hbm, v_hbm, o_hbm, g_hbm, norm_hbm, pos_hbm,
     dq_out, dk_out, dv_out,
     kv, qs, gs, rows_norm, rows_dot, dq_sum, part, part_low, core_in, x_out, x_in, z_out, z_in,
-    kv_done, kv_in, dq_low,
+    kv_done, kv_in, dq_low, q_ref, o_ref, g_ref, norm_ref, pos_ref,
     gz_send, gz_recv, gx_send, gx_recv, gc_send, gc_recv,
-    rc_send, rc_recv, rx_send, rx_recv, rz_send, rz_recv, y_send, y_recv,
+    rc_send, rc_recv, rx_send, rx_recv, rz_send, rz_recv, y_send, y_recv, load_sem,
 ):
-    rows, head = k_ref.shape
+    rows, head = k_hbm.shape
     half = rows // 2
-    runs = zs * xs * 2 * 2
+    chips = zs * xs
+    runs = chips * 2 * 2
     scale = head ** -0.5
     s = lax.axis_index("section")
     me = lax.axis_index("ctx")
@@ -61,18 +62,6 @@
     before = (shift(s, -1, sections), me)
     after = (shift(s, 1, sections), me)
 
-    def send(src, dst, send_sem, recv_sem, to):
-        copy = pltpu.make_async_remote_copy(
-            src_ref=src, dst_ref=dst, send_sem=send_sem, recv_sem=recv_sem,
-            device_id=to, device_id_type=MESH,
-        )
-        return copy
-
-    kv[chip, c, 0:rows] = k_ref[...]
-    kv[chip, c, rows:2 * rows] = v_ref[...]
-    run = lax.shift_right_logical(pos_ref[0:1, 0:1], half.bit_length() - 1).astype(jnp.float32)
-    kv[chip, c, 2 * rows:] = jnp.broadcast_to(run, (16, head)).astype(jnp.bfloat16)
-
     barrier = pltpu.get_barrier_semaphore()
     peers = [z_peer(d) for d in range(1, zs)] + [x_peer(d) for d in range(1, xs)]
     peers += [core_peer, before]
@@ -80,37 +69,73 @@
         peers.append(after)
     for peer in peers:
         pl.semaphore_signal(barrier, inc=1, device_id=peer, device_id_type=MESH)
+
+    pairs = [
+        (pos_hbm, pos_ref), (k_hbm, kv.at[chip, c, pl.ds(0, rows)]), (v_hbm, kv.at[chip, c, pl.ds(rows, rows)]),
+        (q_hbm, q_ref), (g_hbm, g_ref), (o_hbm, o_ref), (norm_hbm, norm_ref),
+    ]
+    loads = [pltpu.make_async_copy(src, dst, load_sem.at[i]) for i, (src, dst) in enumerate(pairs)]
+    for load in loads:
+        load.start()
+    for load in loads[:3]:
+        load.wait()
+    run = lax.shift_right_logical(pos_ref[0:1, 0:1], half.bit_length() - 1).astype(jnp.float32)
+    kv[chip, c, 2 * rows:] = jnp.broadcast_to(run, (16, head)).astype(jnp.bfloat16)
     pl.semaphore_wait(barrier, len(peers))
 
-    started = []
-
-    def begin(copy):
-        copy.start()
-        started.append(copy)
-        return copy
-
-    def chip_at(dz, dx):
+    def copy_to(src, dst, send_sem, recv_sem, to):
+        return pltpu.make_async_remote_copy(
+            src_ref=src, dst_ref=dst, send_sem=send_sem, recv_sem=recv_sem,
+            device_id=to, device_id_type=MESH,
+        )
+
+    def source(dz, dx):
         return shift(z, -dz, zs) * xs + shift(x, -dx, xs)
 
-    z_copies = {}
+    def target(dz, dx):
+        return shift(z, dz, zs) * xs + shift(x, dx, xs)
+
+    def gather_z(dz):
+        return copy_to(kv.at[chip, c], kv.at[chip, c], gz_send.at[dz], gz_recv.at[dz], z_peer(dz))
+
+    def gather_x(dz, dx):
+        t = source(dz, 0)
+        return copy_to(kv.at[t, c], kv.at[t, c], gx_send.at[dz, dx], gx_recv.at[dz, dx], x_peer(dx))
+
+    def gather_c(dz, dx):
+        t = source(dz, dx)
+        return copy_to(kv.at[t, c], kv.at[t, c], gc_send.at[dz, dx], gc_recv.at[dz, dx], core_peer)
+
+    def pass_on(dz):
+        for dx in range(1, xs):
+            gather_x(dz, dx).start()
+        gather_c(dz, 0).start()
+
+    def z_service(dz):
+        gather_z(dz).wait_recv()
+        pass_on(dz)
+
+    def x_service(dz):
+        for dx in range(1, xs):
+            gather_x(dz, dx).wait_recv()
+            gather_c(dz, dx).start()
+
+    def reduce_c(dz, dx):
+        t = source(dz, dx)
+        return copy_to(part_low.at[t, 1 - c], core_in.at[t], rc_send.at[dz, dx], rc_recv.at[dz, dx], core_peer)
+
+    def reduce_x(dz, dx):
+        return copy_to(x_out.at[dz, dx], x_in.at[dz, dx], rx_send.at[dz, dx], rx_recv.at[dz, dx], x_peer(-dx))
+
+    def reduce_z(dz):
+        return copy_to(z_out.at[dz], z_in.at[dz], rz_send.at[dz], rz_recv.at[dz], z_peer(-dz))
+
     for dz in range(1, zs):
-        z_copies[dz] = begin(send(kv.at[chip, c], kv.at[chip, c], gz_send.at[dz], gz_recv.at[dz], z_peer(dz)))
-    x_copies, c_copies = {}, {}
-
-    def forward_x(dz):
-        t = chip_at(dz, 0)
-        for dx in range(1, xs):
-            x_copies[dz, dx] = begin(send(
-                kv.at[t, c], kv.at[t, c], gx_send.at[dz, dx], gx_recv.at[dz, dx], x_peer(dx)))
-
-    def forward_c(dz, dx):
-        t = chip_at(dz, dx)
-        c_copies[dz, dx] = begin(send(
-            kv.at[t, c], kv.at[t, c], gc_send.at[dz, dx], gc_recv.at[dz, dx], core_peer))
-
-    forward_x(0)
-    forward_c(0, 0)
-
+        gather_z(dz).start()
+    pass_on(0)
+
+    for load in loads[3:]:
+        load.wait()
     ones = jnp.ones((8, head), jnp.bfloat16)
     for h in range(group):
         cols = slice(h * head, (h + 1) * head)
@@ -123,25 +148,16 @@
         low = (prod - high.astype(jnp.float32)).astype(jnp.bfloat16)
         total = dot(ones, high, NT) + dot(ones, low, NT)
         rows_dot[:, there] = total
-        rows_norm[:, there] = jnp.broadcast_to(norm_ref[h:h + 1, :] * LOG2E, (8, rows))
+        rows_norm[:, there] = jnp.broadcast_to(norm_ref[h] * LOG2E, (8, rows))
     dq_sum[...] = jnp.zeros_like(dq_sum)
-
-    for dz in range(1, zs + 1):
-        if dz < zs:
-            z_copies[dz].wait_recv()
-            forward_x(dz)
-            forward_c(dz, 0)
-        for dx in range(1, xs):
-            x_copies[dz - 1, dx].wait_recv()
-            forward_c(dz - 1, dx)
-    for copy in c_copies.values():
-        copy.wait_recv()
+    x_service(0)
+    z_service(1)
 
     query_pos = pos_ref[...].astype(jnp.float32)
     row_at = lax.broadcasted_iota(jnp.int32, (half, rows), 0).astype(jnp.float32)
     chunks = [(a, min(a + 2, group)) for a in range(0, group, 2)]
 
-    def blocks(t, _):
+    def tile(t):
         keys = kv[t, :, 0:rows].reshape(2 * rows, head)
         values = kv[t, :, rows:2 * rows].reshape(2 * rows, head)
         bias = []
@@ -172,55 +188,103 @@
             part[t, core, rows:] = dv[these]
             part_low[t, core, 0:rows] = dk[these].astype(jnp.bfloat16)
             part_low[t, core, rows:] = dv[these].astype(jnp.bfloat16)
+
+    def place(j):
+        at = lax.rem(j + 1, chips)
+        dz = lax.div(at, xs)
+        r = lax.rem(at, xs)
+        far = lax.div(dz + (zs - 1), zs)
+        return dz, r + far * (xs - 1 - 2 * r), r
+
+    def core_total(dz, dx):
+        t = source(dz, dx)
+        reduce_c(dz, dx).wait_recv()
+        return part[t, c] + core_in[t].astype(jnp.float32)
+
+    def row_total(dz, total):
+        for dx in range(1, xs):
+            reduce_x(dz, dx).wait_recv()
+            total = total + x_in[dz, dx].astype(jnp.float32)
+        return total
+
+    def after_core(dz, dx):
+        total = core_total(dz, dx)
+
+        @pl.when(dx > 0)
+        def _():
+            x_out[dz, dx] = total.astype(jnp.bfloat16)
+            reduce_x(dz, dx).start()
+
+        @pl.when(dx == 0)
+        def _():
+            part[source(dz, 0), c] = total
+
+    def after_row(dz):
+        z_out[dz] = row_total(dz, part[source(dz, 0), c]).astype(jnp.bfloat16)
+        reduce_z(dz).start()
+
+    def step(j, _):
+        dz, dx, r = place(j)
+        row_start = jnp.logical_and(jnp.logical_and(r == 0, dz > 0), dz < zs - 1)
+
+        @pl.when(row_start)
+        def _():
+            z_service(dz + 1)
+
+        gather_c(dz, dx).wait_recv()
+        tile(source(dz, dx))
+        reduce_c(dz, dx).start()
+
+        @pl.when(jnp.logical_or(row_start, j == xs - 2))
+        def _():
+            x_service(dz + 1)
+
+        @pl.when(j > 0)
+        def _():
+            dz1, dx1, _r = place(j - 1)
+            after_core(dz1, dx1)
+
+        @pl.when(j > 1)
+        def _():
+            dz2, dx2, _r = place(j - 2)
+
+            @pl.when(jnp.logical_and(dz2 > 0, dx2 == 0))
+            def _():
+                after_row(dz2)
+
         return 0
 
-    lax.fori_loop(0, zs * xs, blocks, 0)
-
-    core_copies = {}
-    order = [zs - 1 - i for i in range(zs)]
-    for dz in order:
-        for dx in range(xs):
-            t = chip_at(-dz, -dx)
-            core_copies[dz, dx] = begin(send(
-                part_low.at[t, 1 - c], core_in.at[t], rc_send.at[dz, dx], rc_recv.at[dz, dx], core_peer))
+    lax.fori_loop(0, chips, step, 0)
+
     for h in range(group):
         dq_low[:, h * head:(h + 1) * head] = (
             dq_sum[h * rows:(h + 1) * rows] * scale).astype(jnp.bfloat16)
-    dq_copy = begin(send(dq_low, dq_out, y_send.at[0], y_recv.at[0], before))
-
-    rx_copies = {}
-    for dz in order:
-        for dx in range(xs - 1, -1, -1):
-            core_copies[dz, dx].wait_recv()
-            t = chip_at(-dz, -dx)
-            total = part[t, c] + core_in[t].astype(jnp.float32)
-            if dx:
-                x_out[dz, dx] = total.astype(jnp.bfloat16)
-                rx_copies[dz, dx] = begin(send(
-                    x_out.at[dz, dx], x_in.at[dz, dx], rx_send.at[dz, dx], rx_recv.at[dz, dx], x_peer(dx)))
-            else:
-                part[t, c] = total
-    rz_copies = {}
-    for dz in order:
-        total = part[chip_at(-dz, 0), c]
-        for dx in range(1, xs):
-            rx_copies[dz, dx].wait_recv()
-            total = total + x_in[dz, dx].astype(jnp.float32)
-        if dz:
-            z_out[dz] = total.astype(jnp.bfloat16)
-            rz_copies[dz] = begin(send(
-                z_out.at[dz], z_in.at[dz], rz_send.at[dz], rz_recv.at[dz], z_peer(dz)))
+    dq_copy = copy_to(dq_low, dq_out, y_send.at[0], y_recv.at[0], before)
+    dq_copy.start()
+    after_row(zs - 1)
+    total = row_total(0, core_total(0, 0))
     for dz in range(1, zs):
-        rz_copies[dz].wait_recv()
+        reduce_z(dz).wait_recv()
         total = total + z_in[dz].astype(jnp.float32)
     kv_done[...] = total.astype(jnp.bfloat16)
-    kv_copy = begin(send(kv_done, kv_in, y_send.at[1], y_recv.at[1], before))
+    kv_copy = copy_to(kv_done, kv_in, y_send.at[1], y_recv.at[1], before)
+    kv_copy.start()
     kv_copy.wait_recv()
     dk_out[...] = kv_in[0:rows]
     dv_out[...] = kv_in[rows:]
     dq_copy.wait_recv()
-    for copy in started:
-        copy.wait_send()
+    dq_copy.wait_send()
+    kv_copy.wait_send()
+    for dz in range(zs):
+        if dz:
+            gather_z(dz).wait_send()
+            reduce_z(dz).wait_send()
+        for dx in range(xs):
+            if dx:
+                gather_x(dz, dx).wait_send()
+                reduce_x(dz, dx).wait_send()
+            gather_c(dz, dx).wait_send()
+            reduce_c(dz, dx).wait_send()
 
 
 def solution(mesh):
@@ -242,7 +306,7 @@
                 jax.ShapeDtypeStruct((rows, head), bf16),
                 jax.ShapeDtypeStruct((rows, head), bf16),
             ),
-            in_specs=[vmem] * 7,
+            in_specs=[pl.BlockSpec(memory_space=pltpu.HBM)] * 7,
             out_specs=(vmem,) * 3,
             scratch_shapes=[
                 pltpu.VMEM((chips, 2, 2 * rows + 16, head), bf16),
@@ -261,20 +325,25 @@
                 pltpu.VMEM((2 * rows, head), bf16),
                 pltpu.VMEM((2 * rows, head), bf16),
                 pltpu.VMEM((rows, wide), bf16),
+                pltpu.VMEM((rows, wide), bf16),
+                pltpu.VMEM((rows, wide), bf16),
+                pltpu.VMEM((rows, wide), bf16),
+                pltpu.VMEM((group, 1, rows), f32),
+                pltpu.VMEM((1, rows), jnp.int32),
                 dma((zs,)), dma((zs,)),
                 dma((zs, xs)), dma((zs, xs)),
                 dma((zs, xs)), dma((zs, xs)),
                 dma((zs, xs)), dma((zs, xs)),
                 dma((zs, xs)), dma((zs, xs)),
                 dma((zs,)), dma((zs,)),
-                dma((2,)), dma((2,)),
+                dma((2,)), dma((2,)), dma((7,)),
             ],
             compiler_params=pltpu.CompilerParams(
-                collective_id=0, has_side_effects=True, vmem_limit_bytes=48 * 1024 * 1024
+                collective_id=0, has_side_effects=True, vmem_limit_bytes=63 * 1024 * 1024
             ),
         )(
             query_rows[0], key_rows[0], value_rows[0], attn_output[0], grad_output[0],
-            log_normalizer[0], positions.reshape(1, rows),
+            log_normalizer.transpose(1, 0, 2), positions.reshape(1, rows),
         )
         return dq[None], dk[None], dv[None]
 

time: 52.2 us -> 42.7 us (0.82)
  Pallas kernels: 43.6 us -> 38.8 us
  local copies, waits for them, and re-layouts: 7.58 us -> 3.04 us
    pallas_call x1, Pallas kernels: 43.6 us -> 38.8 us  [shards(): pl.pallas_call(functools.partial(kernel, sections, zs, xs, group), out_sh...]
    unnamed x18 -> x7, local copies, waits for them, and re-layouts: 7.58 us -> 3.04 us
where the time goes in v2:
time: 42.7 us; the launch traced here: 42.5 us
  Pallas kernels  38.8 us (91%)
  local copies, waits for them, and re-layouts  3.04 us (7%)
  between operations  0.65 us (2%)
    pallas_call x1, Pallas kernels, shards(): pl.pallas_call(functools.partial(kernel, sections, zs, xs, group), out_sh...  38.8 us
    unnamed x7, local copies, waits for them, and re-layouts  3.04 us

profile of v2, /device:TPU:0, one launch (start us, length us, event | category | flops | bytes accessed | tf_op | source)
XLA Modules:
  0.0 42.5 jit_solution(11675505048752564025)
XLA Ops:
  0.6 38.8 %shard_map.94 = (bf16[128,896]{1,0:T(8,128)(2,1)}, bf16[128,128]{1,0:T(8,128)(2,1)}, bf16[128,128]{1,0:T(8,128)(2,1)}) custom-call(bf16[128,896]{1,0:T(8,128)(2,1)} %bitcast.11, bf16[128,128]{1,0:T(8,128)(2,1)} %bitcast.14, bf16[128,128]{1,0:T(8,128)(2,1)} %bitcast.15, bf16[128,896]{1,0:T(8,128)(2,1)} %bitcast.12, bf16[128,896]{1,0:T(8,128)(2,1)} %bitcast.13, ...), custom_call_target="tpu_custom_call" | custom-call | tf_op jit(solution)/shard_map/pallas_call | solution.py:302
  39.4 0.0 copy-start.1
  39.4 1.6 %copy.13 = bf16[1,128,896]{2,1,0:T(8,128)(2,1)} copy(bf16[1,128,896]{2,1,0:T(8,128)(2,1)} %bitcast.10) | data formatting | bytes 458752
  41.1 0.0 copy-done.1
  41.1 0.0 copy-start
  41.1 0.6 %copy.14 = bf16[1,128,128]{2,1,0:T(8,128)(2,1)} copy(bf16[1,128,128]{2,1,0:T(8,128)(2,1)S(1)} %bitcast.17) | data formatting | bytes 65536
  41.7 0.2 copy-done
  41.9 0.6 %copy.15 = bf16[1,128,128]{2,1,0:T(8,128)(2,1)} copy(bf16[1,128,128]{2,1,0:T(8,128)(2,1)S(1)} %bitcast.16) | data formatting | bytes 65536
Async XLA Ops:
  39.4 1.7 %copy-start.1 = (bf16[128,128]{1,0:T(8,128)(2,1)S(1)}, bf16[128,128]{1,0:T(8,128)(2,1)}, u32[]{:S(2)}) copy-start(bf16[128,128]{1,0:T(8,128)(2,1)} %get-tuple-element.7) | copy-start | bytes 98308
  41.1 0.8 %copy-start = (bf16[128,128]{1,0:T(8,128)(2,1)S(1)}, bf16[128,128]{1,0:T(8,128)(2,1)}, u32[]{:S(2)}) copy-start(bf16[128,128]{1,0:T(8,128)(2,1)} %get-tuple-element.8) | copy-start | bytes 98308

commit v3 on v2

--- a/solution.py
+++ b/solution.py
@@ -29,10 +29,10 @@
     sections, zs, xs, group,
     q_hbm, k_hbm, v_hbm, o_hbm, g_hbm, norm_hbm, pos_hbm,
     dq_out, dk_out, dv_out,
-    kv, qs, gs, rows_norm, rows_dot, dq_sum, part, part_low, core_in, x_out, x_in, z_out, z_in,
-    kv_done, kv_in, dq_low, q_ref, o_ref, g_ref, norm_ref, pos_ref,
+    kv, qs, gs, rows_norm, rows_dot, dq_sum, part, part_low, core_in, x_out, x_in,
+    kv_done, dq_low, q_ref, o_ref, g_ref, norm_ref, pos_ref,
     gz_send, gz_recv, gx_send, gx_recv, gc_send, gc_recv,
-    rc_send, rc_recv, rx_send, rx_recv, rz_send, rz_recv, y_send, y_recv, load_sem,
+    rc_send, rc_recv, rx_send, rx_recv, y_send, y_recv, load_sem,
 ):
     rows, head = k_hbm.shape
     half = rows // 2
@@ -58,12 +58,15 @@
     def x_peer(d):
         return device(z, shift(x, d, xs), c)
 
+    def direct(dz, dx):
+        return device(shift(z, dz, zs), shift(x, dx, xs), c)
+
     core_peer = device(z, x, 1 - c)
     before = (shift(s, -1, sections), me)
     after = (shift(s, 1, sections), me)
 
     barrier = pltpu.get_barrier_semaphore()
-    peers = [z_peer(d) for d in range(1, zs)] + [x_peer(d) for d in range(1, xs)]
+    peers = [direct(dz, dx) for dz in range(zs) for dx in range(xs) if dz or dx]
     peers += [core_peer, before]
     if sections > 2:
         peers.append(after)
@@ -125,10 +128,7 @@
         return copy_to(part_low.at[t, 1 - c], core_in.at[t], rc_send.at[dz, dx], rc_recv.at[dz, dx], core_peer)
 
     def reduce_x(dz, dx):
-        return copy_to(x_out.at[dz, dx], x_in.at[dz, dx], rx_send.at[dz, dx], rx_recv.at[dz, dx], x_peer(-dx))
-
-    def reduce_z(dz):
-        return copy_to(z_out.at[dz], z_in.at[dz], rz_send.at[dz], rz_recv.at[dz], z_peer(-dz))
+        return copy_to(x_out.at[dz, dx], x_in.at[dz, dx], rx_send.at[dz, dx], rx_recv.at[dz, dx], direct(-dz, -dx))
 
     for dz in range(1, zs):
         gather_z(dz).start()
@@ -193,64 +193,44 @@
         at = lax.rem(j + 1, chips)
         dz = lax.div(at, xs)
         r = lax.rem(at, xs)
-        far = lax.div(dz + (zs - 1), zs)
-        return dz, r + far * (xs - 1 - 2 * r), r
+        last = lax.div(dz, zs - 1)
+        return dz, r + last * (xs - 1 - 2 * r), r
 
     def core_total(dz, dx):
         t = source(dz, dx)
         reduce_c(dz, dx).wait_recv()
         return part[t, c] + core_in[t].astype(jnp.float32)
 
-    def row_total(dz, total):
-        for dx in range(1, xs):
-            reduce_x(dz, dx).wait_recv()
-            total = total + x_in[dz, dx].astype(jnp.float32)
-        return total
-
     def after_core(dz, dx):
-        total = core_total(dz, dx)
-
-        @pl.when(dx > 0)
-        def _():
-            x_out[dz, dx] = total.astype(jnp.bfloat16)
-            reduce_x(dz, dx).start()
-
-        @pl.when(dx == 0)
-        def _():
-            part[source(dz, 0), c] = total
-
-    def after_row(dz):
-        z_out[dz] = row_total(dz, part[source(dz, 0), c]).astype(jnp.bfloat16)
-        reduce_z(dz).start()
+        x_out[dz, dx] = core_total(dz, dx).astype(jnp.bfloat16)
+        reduce_x(dz, dx).start()
 
     def step(j, _):
         dz, dx, r = place(j)
-        row_start = jnp.logical_and(jnp.logical_and(r == 0, dz > 0), dz < zs - 1)
-
-        @pl.when(row_start)
-        def _():
-            z_service(dz + 1)
-
         gather_c(dz, dx).wait_recv()
         tile(source(dz, dx))
         reduce_c(dz, dx).start()
 
-        @pl.when(jnp.logical_or(row_start, j == xs - 2))
+        @pl.when(j == xs - 2)
+        def _():
+            z_service(2)
+
+        @pl.when(jnp.logical_and(r == 0, jnp.logical_and(dz > 0, dz < zs - 2)))
+        def _():
+            z_service(dz + 2)
+
+        @pl.when(jnp.logical_and(r == xs - 1, dz < zs - 2))
         def _():
             x_service(dz + 1)
 
-        @pl.when(j > 0)
-        def _():
-            dz1, dx1, _r = place(j - 1)
-            after_core(dz1, dx1)
+        @pl.when(jnp.logical_and(r == 0, dz == zs - 2))
+        def _():
+            x_service(dz + 1)
 
         @pl.when(j > 1)
         def _():
             dz2, dx2, _r = place(j - 2)
-
-            @pl.when(jnp.logical_and(dz2 > 0, dx2 == 0))
-            def _():
-                after_row(dz2)
+            after_core(dz2, dx2)
 
         return 0
 
@@ -261,30 +241,37 @@
             dq_sum[h * rows:(h + 1) * rows] * scale).astype(jnp.bfloat16)
     dq_copy = copy_to(dq_low, dq_out, y_send.at[0], y_recv.at[0], before)
     dq_copy.start()
-    after_row(zs - 1)
-    total = row_total(0, core_total(0, 0))
-    for dz in range(1, zs):
-        reduce_z(dz).wait_recv()
-        total = total + z_in[dz].astype(jnp.float32)
+    after_core(zs - 1, 0)
+    total = core_total(0, 0)
+    for dz in range(zs):
+        for dx in range(xs):
+            if dz or dx:
+                reduce_x(dz, dx).wait_recv()
+                total = total + x_in[dz, dx].astype(jnp.float32)
     kv_done[...] = total.astype(jnp.bfloat16)
-    kv_copy = copy_to(kv_done, kv_in, y_send.at[1], y_recv.at[1], before)
-    kv_copy.start()
-    kv_copy.wait_recv()
-    dk_out[...] = kv_in[0:rows]
-    dv_out[...] = kv_in[rows:]
-    dq_copy.wait_recv()
-    dq_copy.wait_send()
-    kv_copy.wait_send()
+    dk_copy = copy_to(kv_done.at[pl.ds(0, rows)], dk_out, y_send.at[1], y_recv.at[1], before)
+    dv_copy = copy_to(kv_done.at[pl.ds(rows, rows)], dv_out, y_send.at[2], y_recv.at[2], before)
+    dk_copy.start()
+    dv_copy.start()
+    for copy in (dq_copy, dk_copy, dv_copy):
+        copy.wait_recv()
+        copy.wait_send()
     for dz in range(zs):
         if dz:
             gather_z(dz).wait_send()
-            reduce_z(dz).wait_send()
         for dx in range(xs):
             if dx:
                 gather_x(dz, dx).wait_send()
-                reduce_x(dz, dx).wait_send()
             gather_c(dz, dx).wait_send()
             reduce_c(dz, dx).wait_send()
+            if dz or dx:
+                reduce_x(dz, dx).wait_send()
+
+
+def finish(dq, dk, dv, dq_out, dk_out, dv_out):
+    dq_out[...] = dq[...]
+    dk_out[...] = dk[...]
+    dv_out[...] = dv[...]
 
 
 def solution(mesh):
@@ -298,7 +285,7 @@
         chips = zs * xs
         bf16, f32 = jnp.bfloat16, jnp.float32
         dma = pltpu.SemaphoreType.DMA
-        vmem = pl.BlockSpec(memory_space=pltpu.VMEM)
+        hbm = pl.BlockSpec(memory_space=pltpu.HBM)
         dq, dk, dv = pl.pallas_call(
             functools.partial(kernel, sections, zs, xs, group),
             out_shape=(
@@ -306,8 +293,8 @@
                 jax.ShapeDtypeStruct((rows, head), bf16),
                 jax.ShapeDtypeStruct((rows, head), bf16),
             ),
-            in_specs=[pl.BlockSpec(memory_space=pltpu.HBM)] * 7,
-            out_specs=(vmem,) * 3,
+            in_specs=[hbm] * 7,
+            out_specs=(hbm,) * 3,
             scratch_shapes=[
                 pltpu.VMEM((chips, 2, 2 * rows + 16, head), bf16),
                 pltpu.VMEM((group * rows, head), bf16),
@@ -320,9 +307,6 @@
                 pltpu.VMEM((chips, 2 * rows, head), bf16),
                 pltpu.VMEM((zs, xs, 2 * rows, head), bf16),
                 pltpu.VMEM((zs, xs, 2 * rows, head), bf16),
-                pltpu.VMEM((zs, 2 * rows, head), bf16),
-                pltpu.VMEM((zs, 2 * rows, head), bf16),
-                pltpu.VMEM((2 * rows, head), bf16),
                 pltpu.VMEM((2 * rows, head), bf16),
                 pltpu.VMEM((rows, wide), bf16),
                 pltpu.VMEM((rows, wide), bf16),
@@ -335,8 +319,7 @@
                 dma((zs, xs)), dma((zs, xs)),
                 dma((zs, xs)), dma((zs, xs)),
                 dma((zs, xs)), dma((zs, xs)),
-                dma((zs,)), dma((zs,)),
-                dma((2,)), dma((2,)), dma((7,)),
+                dma((3,)), dma((3,)), dma((7,)),
             ],
             compiler_params=pltpu.CompilerParams(
                 collective_id=0, has_side_effects=True, vmem_limit_bytes=63 * 1024 * 1024
@@ -345,6 +328,17 @@
             query_rows[0], key_rows[0], value_rows[0], attn_output[0], grad_output[0],
             log_normalizer.transpose(1, 0, 2), positions.reshape(1, rows),
         )
+        vmem = pl.BlockSpec(memory_space=pltpu.VMEM)
+        dq, dk, dv = pl.pallas_call(
+            finish,
+            out_shape=(
+                jax.ShapeDtypeStruct((rows, wide), bf16),
+                jax.ShapeDtypeStruct((rows, head), bf16),
+                jax.ShapeDtypeStruct((rows, head), bf16),
+            ),
+            in_specs=[vmem] * 3,
+            out_specs=(vmem,) * 3,
+        )(dq, dk, dv)
         return dq[None], dk[None], dv[None]
 
     return jax.shard_map(

time: 42.7 us -> 39.4 us (0.923)
  local copies, waits for them, and re-layouts: 3.04 us -> 0 us
    unnamed x7 -> x0, local copies, waits for them, and re-layouts: 3.04 us -> none
    pallas_call x1, Pallas kernels: 38.8 us -> 36.9 us  [shards(): pl.pallas_call(functools.partial(kernel, sections, zs, xs, group), out_sh...]
    pallas_call x0 -> x1, Pallas kernels: none -> 1.67 us  [shards(): pl.pallas_call(finish, out_shape=(jax.ShapeDtypeStruct((rows, wide), bf16...]
where the time goes in v3:
time: 39.4 us; the launch traced here: 39.2 us
  Pallas kernels  38.6 us (98%)
  between operations  0.64 us (2%)
    pallas_call x1, Pallas kernels, shards(): pl.pallas_call(functools.partial(kernel, sections, zs, xs, group), out_sh...  36.9 us
    pallas_call x1, Pallas kernels, shards(): pl.pallas_call(finish, out_shape=(jax.ShapeDtypeStruct((rows, wide), bf16...  1.67 us

profile of v3, /device:TPU:0, one launch (start us, length us, event | category | flops | bytes accessed | tf_op | source)
XLA Modules:
  0.0 39.2 jit_solution(5261382668225703789)
XLA Ops:
  0.6 36.9 %shard_map.94 = (bf16[128,896]{1,0:T(8,128)(2,1)}, bf16[128,128]{1,0:T(8,128)(2,1)}, bf16[128,128]{1,0:T(8,128)(2,1)}) custom-call(bf16[128,896]{1,0:T(8,128)(2,1)} %bitcast.10, bf16[128,128]{1,0:T(8,128)(2,1)} %bitcast.13, bf16[128,128]{1,0:T(8,128)(2,1)} %bitcast.14, bf16[128,896]{1,0:T(8,128)(2,1)} %bitcast.11, bf16[128,896]{1,0:T(8,128)(2,1)} %bitcast.12, ...), custom_call_target="tpu_custom_call" | custom-call | tf_op jit(solution)/shard_map/pallas_call | solution.py:289
  37.5 1.7 %shard_map.95 = (bf16[128,896]{1,0:T(8,128)(2,1)}, bf16[128,128]{1,0:T(8,128)(2,1)}, bf16[128,128]{1,0:T(8,128)(2,1)}) custom-call(bf16[128,896]{1,0:T(8,128)(2,1)} %get-tuple-element.9.dq, bf16[128,128]{1,0:T(8,128)(2,1)} %get-tuple-element.10.dk, bf16[128,128]{1,0:T(8,128)(2,1)} %get-tuple-element.11.dv), custom_call_target="tpu_custom_call" | custom-call | tf_op jit(solution)/shard_map/pallas_call | solution.py:332

commit v4 on v3

--- a/solution.py
+++ b/solution.py
@@ -227,9 +227,9 @@
         def _():
             x_service(dz + 1)
 
-        @pl.when(j > 1)
-        def _():
-            dz2, dx2, _r = place(j - 2)
+        @pl.when(j > 0)
+        def _():
+            dz2, dx2, _r = place(j - 1)
             after_core(dz2, dx2)
 
         return 0
@@ -241,7 +241,6 @@
             dq_sum[h * rows:(h + 1) * rows] * scale).astype(jnp.bfloat16)
     dq_copy = copy_to(dq_low, dq_out, y_send.at[0], y_recv.at[0], before)
     dq_copy.start()
-    after_core(zs - 1, 0)
     total = core_total(0, 0)
     for dz in range(zs):
         for dx in range(xs):

time: 39.4 us -> 37.8 us (0.959)
  Pallas kernels: 38.6 us -> 37 us
    pallas_call x1, Pallas kernels: 36.9 us -> 35.3 us  [shards(): pl.pallas_call(functools.partial(kernel, sections, zs, xs, group), out_sh...]
where the time goes in v4:
time: 37.8 us; the launch traced here: 37.6 us
  Pallas kernels  37 us (98%)
  between operations  0.64 us (2%)
    pallas_call x1, Pallas kernels, shards(): pl.pallas_call(functools.partial(kernel, sections, zs, xs, group), out_sh...  35.3 us
    pallas_call x1, Pallas kernels, shards(): pl.pallas_call(finish, out_shape=(jax.ShapeDtypeStruct((rows, wide), bf16...  1.67 us

profile of v4, /device:TPU:0, one launch (start us, length us, event | category | flops | bytes accessed | tf_op | source)
XLA Modules:
  0.0 37.6 jit_solution(10618950342121949699)
XLA Ops:
  0.6 35.3 %shard_map.94 = (bf16[128,896]{1,0:T(8,128)(2,1)}, bf16[128,128]{1,0:T(8,128)(2,1)}, bf16[128,128]{1,0:T(8,128)(2,1)}) custom-call(bf16[128,896]{1,0:T(8,128)(2,1)} %bitcast.10, bf16[128,128]{1,0:T(8,128)(2,1)} %bitcast.13, bf16[128,128]{1,0:T(8,128)(2,1)} %bitcast.14, bf16[128,896]{1,0:T(8,128)(2,1)} %bitcast.11, bf16[128,896]{1,0:T(8,128)(2,1)} %bitcast.12, ...), custom_call_target="tpu_custom_call" | custom-call | tf_op jit(solution)/shard_map/pallas_call | solution.py:288
  36.0 1.7 %shard_map.95 = (bf16[128,896]{1,0:T(8,128)(2,1)}, bf16[128,128]{1,0:T(8,128)(2,1)}, bf16[128,128]{1,0:T(8,128)(2,1)}) custom-call(bf16[128,896]{1,0:T(8,128)(2,1)} %get-tuple-element.9.dq, bf16[128,128]{1,0:T(8,128)(2,1)} %get-tuple-element.10.dk, bf16[128,128]{1,0:T(8,128)(2,1)} %get-tuple-element.11.dv), custom_call_target="tpu_custom_call" | custom-call | tf_op jit(solution)/shard_map/pallas_call | solution.py:331
